TPU v7x, 32 devices: a whole 2x2x4 slice. The times are simulated.
32 devices in a mesh: shard: 8 (over z, x), replica: 4 (over y, core).
Axes of the slice: x: 2, y: 2, z: 4, core: 2. Of those that a mesh axis runs over, the one named last changes fastest.
Arguments:
- kv_grads: bfloat16 [32, 2, 2048, 1024], P(('shard', 'replica')), may hold values from -28800 to 28800
- router_grads: bfloat16 [32, 2, 2048, 8], P(('shard', 'replica')), may hold values from -1536 to 1536
- gain_grads: bfloat16 [32, 2, 2, 2048], P(('shard', 'replica')), may hold values from -1536 to 1536
- kv_master: float32 [2048, 1024], P('shard'), may hold values from -1.5 to 1.5
- kv_first: float32 [2048, 1024], P('shard'), may hold values from -4 to 4
- kv_second: float32 [2048, 1024], P('shard'), may hold values from 0.05 to 2
- router_master: float32 [2048, 8], P('shard'), may hold values from -1.5 to 1.5
- router_first: float32 [2048, 8], P('shard'), may hold values from -4 to 4
- router_second: float32 [2048, 8], P('shard'), may hold values from 0.05 to 2
- gains: float32 [2, 2048], P(None, 'shard'), may hold values from 0.5 to 1.5
- gains_first: float32 [2, 2048], P(None, 'shard'), may hold values from -4 to 4
- gains_second: float32 [2, 2048], P(None, 'shard'), may hold values from 0.05 to 2
Outputs:
- kv_master_new: float32 [2048, 1024], P('shard')
- kv_first_new: float32 [2048, 1024], P('shard')
- kv_second_new: float32 [2048, 1024], P('shard')
- router_master_new: float32 [2048, 8], P('shard')
- router_first_new: float32 [2048, 8], P('shard')
- router_second_new: float32 [2048, 8], P('shard')
- gains_new: float32 [2, 2048], P(None, 'shard')
- gains_first_new: float32 [2, 2048], P(None, 'shard')
- gains_second_new: float32 [2, 2048], P(None, 'shard')
- kv_full: bfloat16 [2048, 1024], replicated
All inputs are finite; a program needn't handle non-finite values.
Results may differ from a plain program's by a relative error of at most 0.0004.
Values may be sent and summed in bfloat16 or wider, within the bound.
A program may use at most 64 MiB of HBM per device.

v0:
```python
import jax
import jax.numpy as jnp
from jax import lax
from jax.sharding import PartitionSpec as P

STEP = 10
PARAMS = 2117632


beta_one = 0.9
beta_two = 0.95
learning_rate = 0.01
adam_eps = 1e-08


def adamw(master, first, second, gradient, weight_decay):
    first_new = beta_one * first + (1.0 - beta_one) * gradient
    second_new = beta_two * second + (1.0 - beta_two) * gradient * gradient
    direction = (
        first_new
        / (1.0 - beta_one**STEP)
        / (jnp.sqrt(second_new / (1.0 - beta_two**STEP)) + adam_eps)
    )
    master_new = master - learning_rate * (direction + weight_decay * master)
    return (master_new, first_new, second_new)


def on_device(
    kv_grads,
    router_grads,
    gain_grads,
    kv_master,
    kv_first,
    kv_second,
    router_master,
    router_first,
    router_second,
    gains,
    gains_first,
    gains_second,
):
    kv_local = kv_grads[0]
    router_term = jnp.sum(router_grads[0].astype(jnp.float32), axis=0)
    gain_term = jnp.sum(gain_grads[0].astype(jnp.float32), axis=0)
    router_part = lax.psum_scatter(router_term, "shard", scatter_dimension=0, tiled=True)
    gain_part = lax.psum_scatter(gain_term, "shard", scatter_dimension=1, tiled=True)
    kv_part = lax.psum_scatter(
        jnp.sum(kv_local.astype(jnp.float32), axis=0), "shard", scatter_dimension=0, tiled=True
    )
    kv_grad, router_grad, gain_grad = lax.psum((kv_part, router_part, gain_part), "replica")
    local_squares = (
        jnp.sum(kv_grad * kv_grad)
        + jnp.sum(router_grad * router_grad)
        + jnp.sum(gain_grad * gain_grad)
    )
    sum_squares = lax.psum(local_squares, "shard")
    clip_factor = jnp.minimum(
        jnp.float32(1.0), jnp.sqrt(jnp.float32(PARAMS)) / (jnp.sqrt(sum_squares) + 1e-06)
    )
    kv_new, kv_first_new, kv_second_new = adamw(
        kv_master, kv_first, kv_second, clip_factor * kv_grad, 0.1
    )
    kv_full = lax.all_gather(kv_new.astype(jnp.bfloat16), "shard", axis=0, tiled=True)
    router_new, router_first_new, router_second_new = adamw(
        router_master, router_first, router_second, clip_factor * router_grad, 0.1
    )
    gains_new, gains_first_new, gains_second_new = adamw(
        gains, gains_first, gains_second, clip_factor * gain_grad, 0.0
    )
    return (
        kv_new,
        kv_first_new,
        kv_second_new,
        router_new,
        router_first_new,
        router_second_new,
        gains_new,
        gains_first_new,
        gains_second_new,
        kv_full,
    )


def solution(mesh):
    placed = (
        P(("shard", "replica"), None, None, None),
        P(("shard", "replica"), None, None, None),
        P(("shard", "replica"), None, None, None),
        P("shard", None),
        P("shard", None),
        P("shard", None),
        P("shard", None),
        P("shard", None),
        P("shard", None),
        P(None, "shard"),
        P(None, "shard"),
        P(None, "shard"),
    )
    return jax.shard_map(
        on_device,
        mesh=mesh,
        in_specs=placed,
        out_specs=(
            P("shard", None),
            P("shard", None),
            P("shard", None),
            P("shard", None),
            P("shard", None),
            P("shard", None),
            P(None, "shard"),
            P(None, "shard"),
            P(None, "shard"),
            P(),
        ),
        check_vma=False,
    )
```

profile of v0, /device:TPU:0, one launch (start us, length us, event | category | flops | bytes accessed | tf_op | source)
XLA Modules:
  0.0 449.4 jit_solution(11799813099606208681)
XLA Ops:
  7.2 0.0 reduce-scatter.6.cloned.1.call-start
  7.2 9.8 %convert_reduce_fusion = f32[2048,1024]{1,0:T(8,128)} fusion(bf16[1,2,2048,1024]{3,2,1,0:T(8,128)(2,1)} %param.12), kind=kLoop, calls=%fused_computation | loop fusion | flops 6291456 | bytes 16777216 | tf_op jit(solution)/shard_map/reduce_sum | solution.py:48
  17.1 0.0 reduce-scatter.6.cloned.1.call-update
  17.1 0.0 copy-start.8
  17.1 0.0 copy-start.9
  17.2 0.0 copy-start.6
  17.2 0.0 reduce-scatter.10.cloned.1.call-start
  17.2 0.6 copy-done.4
  17.8 1.3 copy.22
  19.2 0.0 reduce-scatter.10.cloned.1.call-update
  19.2 0.0 reduce-scatter.8.cloned.1.call-start
  19.2 0.6 convert_reduce_fusion.1
  19.9 0.0 reduce-scatter.8.cloned.1.call-update
  19.9 0.0 all-reduce.3.cloned.1.call-start
  20.0 149.0 %reduce-scatter.6.cloned.1.call-done = f32[256,1024]{1,0:T(8,128)} async-done(((f32[2048,1024]{1,0:T(8,128)}), f32[256,1024]{1,0:T(8,128)}) %reduce-scatter.6.cloned.1.call-update) | async-done | bytes 1048592 | tf_op jit(solution)/shard_map/reduce_scatter | solution.py:47
  169.0 0.0 all-reduce.3.cloned.1.call-update
  169.0 0.0 all-gather.2.cloned.1.call-start
  169.0 66.8 %reduce-scatter.10.cloned.1.call-done = f32[256,2]{1,0:T(8,128)} async-done(((f32[2048,2]{1,0:T(8,128)}), f32[256,2]{1,0:T(8,128)}) %reduce-scatter.10.cloned.1.call-update) | async-done | bytes 2064
  235.9 1.0 copy.23
  236.8 63.3 %reduce-scatter.8.cloned.1.call-done = f32[256,8]{0,1:T(8,128)} async-done(((f32[2048,8]{0,1:T(8,128)}), f32[256,8]{0,1:T(8,128)}) %reduce-scatter.8.cloned.1.call-update) | async-done | bytes 8208 | tf_op jit(solution)/shard_map/reduce_scatter | solution.py:45
  300.1 10.5 %all-reduce = (f32[256,8]{0,1:T(8,128)S(1)}, f32[2,256]{1,0:T(2,128)S(1)}) all-reduce(f32[256,8]{0,1:T(8,128)} %reduce-scatter.8.cloned.1.call-done, f32[2,256]{1,0:T(2,128)S(1)} %copy.23), channel_id=1, replica_groups=mesh['shard'=8,'replica'=4] {'replica'}, use_global_device_ids=true, to_apply=%region_6.0 | all-reduce | flops 2560 | bytes 20480 | tf_op jit(solution)/shard_map/psum | solution.py:50
  310.7 0.6 multiply_reduce_fusion.2
  311.3 0.6 multiply_reduce_fusion.1
  311.9 25.6 %all-reduce.3.cloned.1.call-done = f32[256,1024]{1,0:T(8,128)} async-done(((f32[256,1024]{1,0:T(8,128)}), f32[256,1024]{1,0:T(8,128)}) %all-reduce.3.cloned.1.call-update) | async-done | bytes 1048592 | tf_op jit(solution)/shard_map/psum | solution.py:50
  337.5 2.1 multiply_reduce_fusion
  341.5 21.9 %psum.31 = f32[]{:T(128)} all-reduce(f32[]{:T(128)S(6)} %add.69), channel_id=1, replica_groups=mesh['shard'=8,'replica'=4] {'shard'}, use_global_device_ids=true, to_apply=%region_12.0 | all-reduce | flops 1 | bytes 8 | tf_op jit(solution)/shard_map/psum | solution.py:56
  364.1 3.8 fusion.3
  367.9 0.0 all-gather.2.cloned.1.call-update
  368.0 0.6 multiply_subtract_fusion.2
  368.6 0.6 multiply_subtract_fusion.1
  369.2 69.0 %all-gather.2.cloned.1.call-done = bf16[2048,1024]{1,0:T(8,128)(2,1)} async-done(((bf16[256,1024]{1,0:T(8,128)(2,1)}), bf16[2048,1024]{1,0:T(8,128)(2,1)}) %all-gather.2.cloned.1.call-update) | async-done | bytes 4194320 | tf_op jit(solution)/shard_map/all_gather | solution.py:63
  438.3 4.6 %copy.26 = bf16[2048,1024]{1,0:T(8,128)(2,1)} copy(bf16[2048,1024]{1,0:T(8,128)(2,1)} %all-gather.2.cloned.1.call-done) | data formatting | bytes 8388608
  (19 shorter events, 0.1 us)
Async XLA Ops:
  7.2 161.8 %reduce-scatter.6.cloned.1.call-start = ((), (), s32[]{:S(2)}) async-start(), calls=%async_computation.3 | async-start | bytes 9437184 | tf_op jit(solution)/shard_map/reduce_scatter | solution.py:47
  17.1 0.7 copy-start.4
  17.1 2.2 copy-start.3
  17.1 347.0 %copy-start = (f32[256,1024]{1,0:T(8,128)S(1)}, f32[256,1024]{1,0:T(8,128)}, u32[]{:S(2)}) copy-start(f32[256,1024]{1,0:T(8,128)} %param.15) | copy-start | bytes 3145732
  17.1 347.0 %copy-start.1 = (f32[256,1024]{1,0:T(8,128)S(1)}, f32[256,1024]{1,0:T(8,128)}, u32[]{:S(2)}) copy-start(f32[256,1024]{1,0:T(8,128)} %param.16) | copy-start | bytes 3145732
  17.1 347.1 %copy-start.2 = (f32[256,1024]{1,0:T(8,128)S(1)}, f32[256,1024]{1,0:T(8,128)}, u32[]{:S(2)}) copy-start(f32[256,1024]{1,0:T(8,128)} %param.17) | copy-start | bytes 3145732
  17.1 350.8 %copy-start.8 = (f32[2,256]{1,0:T(2,128)S(1)}, f32[2,256]{1,0:T(2,128)}, u32[]{:S(2)}) copy-start(f32[2,256]{1,0:T(2,128)} %param.21) | copy-start | bytes 6148
  17.1 350.8 %copy-start.9 = (f32[2,256]{1,0:T(2,128)S(1)}, f32[2,256]{1,0:T(2,128)}, u32[]{:S(2)}) copy-start(f32[2,256]{1,0:T(2,128)} %param.22) | copy-start | bytes 6148
  17.1 350.8 %copy-start.10 = (f32[2,256]{1,0:T(2,128)S(1)}, f32[2,256]{1,0:T(2,128)}, u32[]{:S(2)}) copy-start(f32[2,256]{1,0:T(2,128)} %param.23) | copy-start | bytes 6148
  17.1 351.5 %copy-start.5 = (f32[256,8]{0,1:T(8,128)S(1)}, f32[256,8]{0,1:T(8,128)}, u32[]{:S(2)}) copy-start(f32[256,8]{0,1:T(8,128)} %param.18) | copy-start | bytes 24580
  17.2 351.4 %copy-start.6 = (f32[256,8]{0,1:T(8,128)S(1)}, f32[256,8]{0,1:T(8,128)}, u32[]{:S(2)}) copy-start(f32[256,8]{0,1:T(8,128)} %param.19) | copy-start | bytes 24580
  17.2 351.4 %copy-start.7 = (f32[256,8]{0,1:T(8,128)S(1)}, f32[256,8]{0,1:T(8,128)}, u32[]{:S(2)}) copy-start(f32[256,8]{0,1:T(8,128)} %param.20) | copy-start | bytes 24580
  17.2 218.7 %reduce-scatter.10.cloned.1.call-start = ((), (), s32[]{:S(2)}) async-start(), calls=%async_computation.7 | async-start | bytes 1179648
  19.2 280.9 %reduce-scatter.8.cloned.1.call-start = ((), (), s32[]{:S(2)}) async-start(), calls=%async_computation.5 | async-start | bytes 73728 | tf_op jit(solution)/shard_map/reduce_scatter | solution.py:45
  19.9 317.6 %all-reduce.3.cloned.1.call-start = ((), (), s32[]{:S(2)}) async-start(), calls=%async_computation.4 | async-start | bytes 2097152 | tf_op jit(solution)/shard_map/psum | solution.py:50
  169.0 269.3 %all-gather.2.cloned.1.call-start = ((), (), s32[]{:S(2)}) async-start(), calls=%async_computation.6 | async-start | bytes 4718592 | tf_op jit(solution)/shard_map/all_gather | solution.py:63
Sparse Core Ops, SparseCore 0:
  17.2 151.6 reduce-scatter.5
  173.3 62.4 reduce-scatter.9
  239.8 60.2 reduce-scatter.7
  302.3 35.0 all-reduce.2
  368.1 70.1 all-gather.1
where the time goes:
time: 450 us; the launch traced here: 449 us
  waiting for transfers between devices  374 us (83%)
  blocking collectives  32.4 us (7%)
  other arithmetic  18.8 us (4%)
  between operations  16.6 us (4%)
  local copies, waits for them, and re-layouts  7.57 us (2%)
    reduce_scatter x1, waiting for transfers between devices, on_device(): lax.psum_scatter(jnp.sum(kv_local.astype(jnp.float32), axis=0), 'shard',...  149 us
    all_gather x1, waiting for transfers between devices, on_device(): lax.all_gather(kv_new.astype(jnp.bfloat16), 'shard', axis=0, tiled=True)  69 us
    unnamed x6, waiting for transfers between devices  66.9 us
    reduce_scatter x1, waiting for transfers between devices, on_device(): lax.psum_scatter(router_term, 'shard', scatter_dimension=0, tiled=True)  63.3 us
    psum x1, waiting for transfers between devices, on_device(): lax.psum((kv_part, router_part, gain_part), 'replica')  25.6 us
    psum x1, blocking collectives, on_device(): sum_squares = lax.psum(local_squares, 'shard')  21.9 us
    psum x1, blocking collectives, on_device(): lax.psum((kv_part, router_part, gain_part), 'replica')  10.5 us
    reduce_sum x1, other arithmetic, on_device(): jnp.sum(kv_local.astype(jnp.float32), axis=0)  9.85 us
  transfers between devices with their start and end apart: 5, of which 5 were waited for; matrix products, arithmetic and copies ran while one was open for 1% of the time, Pallas kernels for 0%

commit v1 on v0

v1 whole, which is shorter than its diff:
```python
import functools
import jax
import jax.numpy as jnp
from jax import lax
from jax.experimental import pallas as pl
from jax.experimental.pallas import tpu as pltpu
from jax.sharding import PartitionSpec as P

STEP = 10
PARAMS = 2117632
CHUNKS = 2

beta_one = 0.9
beta_two = 0.95
learning_rate = 0.01
adam_eps = 1e-08


def adamw(master, first, second, gradient, weight_decay):
    first_new = beta_one * first + (1.0 - beta_one) * gradient
    second_new = beta_two * second + (1.0 - beta_two) * gradient * gradient
    direction = (
        first_new
        / (1.0 - beta_one**STEP)
        / (jnp.sqrt(second_new / (1.0 - beta_two**STEP)) + adam_eps)
    )
    master_new = master - learning_rate * (direction + weight_decay * master)
    return (master_new, first_new, second_new)


def encode(x):
    return ((x * jnp.abs(x)) * (x * x)).astype(jnp.bfloat16)


def decode(code):
    y = code.astype(jnp.float32)
    size = jnp.abs(y)
    x = lax.rsqrt(lax.rsqrt(size))
    x = jnp.where(y < 0, -x, x)
    return jnp.where(size < 2e-38, 0.0, x)


def bit(value, j):
    return lax.rem(lax.div(value, 2**j), 2)


def flipped(value, other, width):
    out = 0
    for j in range(width):
        out = out + lax.rem(bit(value, j) + bit(other, j), 2) * 2**j
    return out


def orders(shard_bits, replica_bits):
    shards = [("shard", j) for j in range(shard_bits)]
    replicas = [("replica", j) for j in range(replica_bits)]
    one = [replicas[0], shards[0]] + replicas[1:] + shards[1:]
    two = replicas + shards
    return (one, two)


def kernel(
    shards, replicas,
    kv_grads, router_grads, gain_grads, master, first, second,
    r_master, r_first, r_second, g_master, g_first, g_second,
    master_out, first_out, second_out, rm_out, rf_out, rs_out, gm_out, gf_out, gs_out, full,
    slabs, acc, outgoing, incoming, whole_sum, own,
    small, small_in, small_out, square_out, square_in,
    load_sem, cut_send, cut_recv, small_send, small_recv, join_send, join_recv,
    square_send, square_recv, up_sem, down_sem, x_sem, pair_sem, local_sem,
):
    s, r = lax.axis_index("shard"), lax.axis_index("replica")
    rows, columns = master.shape
    width = columns // (CHUNKS * replicas)
    small_width = r_master.shape[1]
    shard_bits, replica_bits = shards.bit_length() - 1, replicas.bit_length() - 1
    bits = shard_bits + replica_bits
    blocks = shards * replicas
    plan = orders(shard_bits, replica_bits)
    step = min(rows, 64)
    pieces = [pl.ds(i * step, step) for i in range(rows // step)]

    def partner(axis, j):
        if axis == "shard":
            return {"shard": s + (1 - 2 * bit(s, j)) * 2**j, "replica": r}
        return {"shard": s, "replica": r + (1 - 2 * bit(r, j)) * 2**j}

    def remote(src, dst, send, recv, device):
        return pltpu.make_async_remote_copy(
            src_ref=src, dst_ref=dst, send_sem=send, recv_sem=recv,
            device_id=device, device_id_type=pl.DeviceIdType.MESH,
        )

    def load(offset):
        owner = flipped(s, offset, shard_bits)
        return pltpu.make_async_copy(
            kv_grads.at[:, pl.ds(pl.multiple_of(owner * rows, rows), rows), :],
            slabs.at[offset], load_sem.at[offset],
        )

    pl.loop(0, shards)(lambda offset: load(offset).start())

    lines = shards // 2
    z, x = lax.div(s, 2), lax.rem(s, 2)
    barrier = pltpu.get_barrier_semaphore()
    for axis, j in plan[0]:
        pl.semaphore_signal(
            barrier, inc=1, device_id=partner(axis, j), device_id_type=pl.DeviceIdType.MESH
        )
    above, below = {"shard": s + 2, "replica": r}, {"shard": s - 2, "replica": r}

    @pl.when(z < lines - 1)
    def _():
        pl.semaphore_signal(barrier, inc=1, device_id=above, device_id_type=pl.DeviceIdType.MESH)

    @pl.when(z > 0)
    def _():
        pl.semaphore_signal(barrier, inc=1, device_id=below, device_id_type=pl.DeviceIdType.MESH)

    def column_of(chunk, offset):
        owner = flipped(r, offset, replica_bits)
        return pl.ds(pl.multiple_of((chunk * replicas + owner) * width, width), width)

    def place(chunk, shard_offset, replica_offset):
        out = 0
        for k, (axis, j) in enumerate(plan[chunk]):
            out = out + bit(shard_offset if axis == "shard" else replica_offset, j) * (
                blocks >> (k + 1)
            )
        return out

    def prepare(chunk, sent):
        def body(offset):
            for q in range(replicas):
                if q % 2 != sent:
                    continue
                at = place(chunk, offset, q)
                cols = column_of(chunk, q)
                for piece in pieces:
                    value = slabs[offset, 0, piece, cols].astype(jnp.float32) + slabs[
                        offset, 1, piece, cols
                    ].astype(jnp.float32)
                    if sent:
                        outgoing[chunk, at, piece, :] = encode(value)
                    else:
                        acc[chunk, at, piece, :] = value

        pl.loop(0, shards)(body)

    def cut(chunk, k):
        half = blocks >> (k + 1)
        axis, j = plan[chunk][k]
        return remote(
            outgoing.at[chunk, pl.ds(half, half)], incoming.at[chunk, pl.ds(half, half)],
            cut_send.at[chunk, k], cut_recv.at[chunk, k], partner(axis, j),
        )

    pl.loop(0, shards)(lambda offset: load(offset).wait())
    prepare(0, 1)
    pl.semaphore_wait(
        barrier, bits + jnp.where(z < lines - 1, 1, 0) + jnp.where(z > 0, 1, 0)
    )
    cut(0, 0).start()
    prepare(1, 1)
    cut(1, 0).start()

    small_plan = [("shard", j) for j in range(shard_bits)] + [
        ("replica", j) for j in range(replica_bits)
    ]

    def small_place(offset):
        out = 0
        for k in range(shard_bits):
            out = out + bit(offset, k) * (shards >> (k + 1))
        return out

    def small_body(offset):
        owner = flipped(s, offset, shard_bits)
        at = small_place(offset)
        small[at] = jnp.zeros((16, small_width), jnp.float32)

        def taken(ref):
            if small_width % 128 == 0:
                cols = pl.ds(pl.multiple_of(owner * small_width, small_width), small_width)
                return ref[0, :, cols].astype(jnp.float32) + ref[1, :, cols].astype(jnp.float32)
            total = ref[0].astype(jnp.float32) + ref[1].astype(jnp.float32)
            out = jnp.zeros((total.shape[0], small_width), jnp.float32)
            for i in range(shards):
                out = jnp.where(owner == i, total[:, i * small_width : (i + 1) * small_width], out)
            return out

        small[at, 0:8, :] = taken(router_grads)
        small[at, 8:10, :] = taken(gain_grads)

    pl.loop(0, shards)(small_body)

    def small_copy(k):
        axis, j = small_plan[k]
        if k < shard_bits:
            half = shards >> (k + 1)
            return remote(
                small.at[pl.ds(half, half)], small_in.at[pl.ds(half, half)],
                small_send.at[k], small_recv.at[k], partner(axis, j),
            )
        i = k - shard_bits
        return remote(
            small_out.at[i], small_in.at[shards + i],
            small_send.at[k], small_recv.at[k], partner(axis, j),
        )

    small_copy(0).start()
    prepare(0, 0)
    prepare(1, 0)

    def take(chunk, k):
        half = blocks >> (k + 1)
        cut(chunk, k).wait_recv()
        rest = half // 2

        def send_body(i):
            for piece in pieces:
                outgoing[chunk, i, piece, :] = encode(
                    acc[chunk, i, piece, :] + decode(incoming[chunk, half + i, piece, :])
                )

        def keep_body(i):
            for piece in pieces:
                acc[chunk, i, piece, :] += decode(incoming[chunk, half + i, piece, :])

        if rest:
            pl.loop(rest, half)(send_body)
            cut(chunk, k + 1).start()
            pl.loop(0, rest)(keep_body)
        else:
            for piece in pieces:
                whole_sum[chunk, 0, piece, :] = acc[chunk, 0, piece, :] + decode(
                    incoming[chunk, half, piece, :]
                )

    def take_small(k):
        small_copy(k).wait_recv()
        if k < shard_bits:
            half = shards >> (k + 1)

            def body(i):
                small[i] += small_in[half + i]

            pl.loop(0, half)(body)
            if k == shard_bits - 1:
                small_out[0] = small[0]
        else:
            i = k - shard_bits
            small_out[i + 1] = small_out[i] + small_in[shards + i]
        if k < bits - 1:
            small_copy(k + 1).start()

    join_bits = list(reversed(range(replica_bits)))

    def join(chunk, i):
        known = 2**i
        return remote(
            whole_sum.at[chunk, pl.ds(0, known)], whole_sum.at[chunk, pl.ds(known, known)],
            join_send.at[chunk, i], join_recv.at[chunk, i], partner("replica", join_bits[i]),
        )

    for k in range(bits):
        for chunk in range(CHUNKS):
            take(chunk, k)
            if k == bits - 1:
                join(chunk, 0).start()
        take_small(k)

    def folded(value):
        return jnp.sum(value.reshape(-1, 8, 128), axis=0)

    squares = jnp.zeros((8, 128), jnp.float32)
    for chunk in range(CHUNKS):
        for piece in pieces:
            value = whole_sum[chunk, 0, piece, :]
            squares = squares + folded(value * value)
    small_sum = small_out[replica_bits]
    squares = squares + jnp.sum(small_sum * small_sum) * (1.0 / (replicas * 8 * 128))
    square_out[0] = squares

    def square_copy(k):
        axis, j = small_plan[k]
        return remote(
            square_out.at[k], square_in.at[k], square_send.at[k], square_recv.at[k],
            partner(axis, j),
        )

    for k in range(bits):
        square_copy(k).start()
        square_copy(k).wait_recv()
        square_out[k + 1] = square_out[k] + square_in[k]
    for i in range(1, replica_bits):
        for chunk in range(CHUNKS):
            join(chunk, i - 1).wait_recv()
            join(chunk, i).start()

    total = jnp.broadcast_to(jnp.sum(square_out[bits], keepdims=True), (8, 128))
    clip = jnp.minimum(
        1.0, jnp.sqrt(jnp.full((8, 128), PARAMS, jnp.float32)) / (jnp.sqrt(total) + 1e-06)
    )
    clip = clip[0:1, 0:1]

    rm_out[...], rf_out[...], rs_out[...] = adamw(
        r_master[...], r_first[...], r_second[...], clip * small_sum[0:8], 0.1
    )
    gm_out[...], gf_out[...], gs_out[...] = adamw(
        g_master[...], g_first[...], g_second[...], clip * small_sum[8:10], 0.0
    )

    def replica_offset(at):
        out = 0
        for i, j in enumerate(join_bits):
            out = out + ((at >> i) % 2) * 2**j
        return out

    for at in range(replicas):
        for chunk in range(CHUNKS):
            if at == replicas // 2:
                join(chunk, replica_bits - 1).wait_recv()
            cols = column_of(chunk, replica_offset(at))
            for piece in pieces:
                new, first_new, second_new = adamw(
                    master[piece, cols], first[piece, cols], second[piece, cols],
                    clip * whole_sum[chunk, at, piece, :], 0.1,
                )
                master_out[piece, cols] = new
                first_out[piece, cols] = first_new
                second_out[piece, cols] = second_new
                own[piece, cols] = new.astype(jnp.bfloat16)

    side = lax.rem(r, 2)
    half_columns = columns // 2
    cols = pl.ds(pl.multiple_of(side * half_columns, half_columns), half_columns)
    pair, across = partner("replica", 0), partner("shard", 0)

    def block(zz, xx):
        return full.at[pl.ds(pl.multiple_of((zz * 2 + xx) * rows, rows), rows), cols]

    def up(t):
        src = own.at[:, cols] if isinstance(t, int) else block(z - t, x)
        return remote(src, block(z - t, x), up_sem.at[0, t], up_sem.at[1, t], above)

    def down(t):
        src = own.at[:, cols] if isinstance(t, int) else block(z + t, x)
        return remote(src, block(z + t, x), down_sem.at[0, t], down_sem.at[1, t], below)

    def cross(role, zz):
        src = own.at[:, cols] if isinstance(role, int) else block(zz, x)
        return remote(src, block(zz, x), x_sem.at[0, role], x_sem.at[1, role], across)

    def to_pair(which, role, zz, xx):
        return remote(
            block(zz, xx), block(zz, xx),
            pair_sem.at[0, which, role], pair_sem.at[1, which, role], pair,
        )

    mine = pltpu.make_async_copy(
        own, full.at[pl.ds(pl.multiple_of(s * rows, rows), rows)], local_sem
    )

    @pl.when(z < lines - 1)
    def _():
        up(0).start()

    @pl.when(z > 0)
    def _():
        down(0).start()

    cross(0, z).start()
    mine.start()
    cross(0, z).wait_recv()
    to_pair(1, 0, z, 1 - x).start()

    def walk(t):
        @pl.when(z - t >= 0)
        def _():
            up(t - 1).wait_recv()

            @pl.when(z < lines - 1)
            def _():
                up(t).start()

            cross(t, z - t).start()
            to_pair(0, t, z - t, x).start()

        @pl.when(z + t < lines)
        def _():
            down(t - 1).wait_recv()

            @pl.when(z > 0)
            def _():
                down(t).start()

            cross(lines + t, z + t).start()
            to_pair(0, lines + t, z + t, x).start()

        @pl.when(z - t >= 0)
        def _():
            cross(t, z - t).wait_recv()
            to_pair(1, t, z - t, 1 - x).start()

        @pl.when(z + t < lines)
        def _():
            cross(lines + t, z + t).wait_recv()
            to_pair(1, lines + t, z + t, 1 - x).start()

    pl.loop(1, lines)(walk)

    mine.wait()
    cross(0, z).wait_send()
    to_pair(1, 0, z, 1 - x).wait()

    @pl.when(z < lines - 1)
    def _():
        up(0).wait_send()

    @pl.when(z > 0)
    def _():
        down(0).wait_send()

    def settle(t):
        @pl.when(z - t >= 0)
        def _():
            @pl.when(z < lines - 1)
            def _():
                up(t).wait_send()

            cross(t, z - t).wait_send()
            to_pair(0, t, z - t, x).wait()
            to_pair(1, t, z - t, 1 - x).wait()

        @pl.when(z + t < lines)
        def _():
            @pl.when(z > 0)
            def _():
                down(t).wait_send()

            cross(lines + t, z + t).wait_send()
            to_pair(0, lines + t, z + t, x).wait()
            to_pair(1, lines + t, z + t, 1 - x).wait()

    pl.loop(1, lines)(settle)
    for k in range(bits):
        for chunk in range(CHUNKS):
            cut(chunk, k).wait_send()
        small_copy(k).wait_send()
        square_copy(k).wait_send()
    for i in range(replica_bits):
        for chunk in range(CHUNKS):
            join(chunk, i).wait_send()


def on_device(
    shards, replicas,
    kv_grads, router_grads, gain_grads,
    kv_master, kv_first, kv_second,
    router_master, router_first, router_second,
    gains, gains_first, gains_second,
):
    rows, columns = kv_master.shape
    blocks = shards * replicas
    bits = blocks.bit_length() - 1
    replica_bits = replicas.bit_length() - 1
    width = columns // (CHUNKS * replicas)
    small_width = router_master.shape[0]
    lines = shards // 2
    f32, bf16 = jnp.float32, jnp.bfloat16
    shape = jax.ShapeDtypeStruct
    vmem, anywhere = pl.BlockSpec(memory_space=pltpu.VMEM), pl.BlockSpec(memory_space=pl.ANY)
    dma = pltpu.SemaphoreType.DMA
    outs = pl.pallas_call(
        functools.partial(kernel, shards, replicas),
        out_shape=[shape(kv_master.shape, f32)] * 3
        + [shape(router_master.shape[::-1], f32)] * 3
        + [shape(gains.shape, f32)] * 3
        + [shape((rows * shards, columns), bf16)],
        in_specs=[anywhere] + [vmem] * 11,
        out_specs=[vmem] * 9 + [anywhere],
        scratch_shapes=[
            pltpu.VMEM((shards, 2, rows, columns), bf16),
            pltpu.VMEM((CHUNKS, blocks // 2, rows, width), f32),
            pltpu.VMEM((CHUNKS, blocks, rows, width), bf16),
            pltpu.VMEM((CHUNKS, blocks, rows, width), bf16),
            pltpu.VMEM((CHUNKS, replicas, rows, width), f32),
            pltpu.VMEM((rows, columns), bf16),
            pltpu.VMEM((shards, 16, small_width), f32),
            pltpu.VMEM((shards + replica_bits, 16, small_width), f32),
            pltpu.VMEM((replica_bits + 1, 16, small_width), f32),
            pltpu.VMEM((bits + 1, 8, 128), f32),
            pltpu.VMEM((bits, 8, 128), f32),
            dma((shards,)),
            dma((CHUNKS, bits)), dma((CHUNKS, bits)),
            dma((bits,)), dma((bits,)),
            dma((CHUNKS, replica_bits)), dma((CHUNKS, replica_bits)),
            dma((bits,)), dma((bits,)),
            dma((2, lines)), dma((2, lines)),
            dma((2, 2 * lines)),
            dma((2, 2, 2 * lines)),
            dma,
        ],
        compiler_params=pltpu.CompilerParams(
            collective_id=0, has_side_effects=True, vmem_limit_bytes=52 * 2**20
        ),
    )(
        kv_grads[0], router_grads[0].transpose(0, 2, 1), gain_grads[0],
        kv_master, kv_first, kv_second,
        router_master.T, router_first.T, router_second.T,
        gains, gains_first, gains_second,
    )
    return (*outs[:3], *(out.T for out in outs[3:6]), *outs[6:])


def solution(mesh):
    kept, gain_split = P("shard", None), P(None, "shard")
    grads = P(("shard", "replica"), None, None, None)
    return jax.shard_map(
        functools.partial(on_device, mesh.shape["shard"], mesh.shape["replica"]),
        mesh=mesh,
        in_specs=(grads,) * 3 + (kept,) * 6 + (gain_split,) * 3,
        out_specs=(kept,) * 6 + (gain_split,) * 3 + (P(),),
        check_vma=False,
    )
```

time: 450 us -> 115 us (0.26)
  waiting for transfers between devices: 374 us -> 0 us
  Pallas kernels: 0 us -> 96 us
  blocking collectives: 32.4 us -> 0 us
  other arithmetic: 18.8 us -> 0 us
  between operations: 16.6 us -> 0.68 us
  local copies, waits for them, and re-layouts: 7.57 us -> 17.5 us
    reduce_scatter x2 -> x0, waiting for transfers between devices: 212 us -> none  [the longest x1 149 us: on_device(): lax.psum_scatter(jnp.sum(kv_local.astype(jnp.float32), axis=0), 'shard',...]
    pallas_call x0 -> x1, Pallas kernels: none -> 96 us  [on_device(): pl.pallas_call(functools.partial(kernel, shards, replicas), out_shape=[sh...]
    all_gather x1 -> x0, waiting for transfers between devices: 69 us -> none  [on_device(): lax.all_gather(kv_new.astype(jnp.bfloat16), 'shard', axis=0, tiled=True)]
    unnamed x6 -> x0, waiting for transfers between devices: 66.9 us -> none
    psum x2 -> x0, blocking collectives: 32.4 us -> none  [the longest x1 21.9 us: on_device(): sum_squares = lax.psum(local_squares, 'shard')]
    psum x1 -> x0, waiting for transfers between devices: 25.6 us -> none  [on_device(): lax.psum((kv_part, router_part, gain_part), 'replica')]
    reduce_sum x6 -> x0, other arithmetic: 13.8 us -> none  [the longest x1 9.85 us: on_device(): jnp.sum(kv_local.astype(jnp.float32), axis=0)]
    unnamed x25 -> x28, local copies, waits for them, and re-layouts: 7.57 us -> 17.5 us
  transfers between devices with their start and end apart: 5 -> 0, of which waited for: 5 -> 0; matrix products, arithmetic and copies ran while one was open for 1% -> 0% of each run, Pallas kernels for 0% -> 0%
where the time goes in v1:
time: 115 us; the launch traced here: 114 us
  Pallas kernels  96 us (83%)
  local copies, waits for them, and re-layouts  17.5 us (15%)
    pallas_call x1, Pallas kernels, on_device(): pl.pallas_call(functools.partial(kernel, shards, replicas), out_shape=[sh...  96 us
    unnamed x28, local copies, waits for them, and re-layouts  17.5 us

profile of v1, /device:TPU:0, one launch (start us, length us, event | category | flops | bytes accessed | tf_op | source)
XLA Modules:
  0.0 114.1 jit_solution(14240180418368826887)
XLA Ops:
  0.6 0.0 copy-start
  0.7 0.8 copy-done
  1.5 0.0 copy-start.1
  1.5 0.7 copy-done.1
  2.2 0.0 copy-start.2
  2.2 0.7 copy-done.2
  2.9 0.0 copy-start.3
  2.9 0.7 copy-done.3
  3.6 0.0 copy-start.4
  3.6 0.7 copy-done.4
  4.3 0.0 copy-start.5
  4.3 0.7 copy-done.5
  5.0 0.0 copy-start.6
  5.0 0.7 copy-done.6
  5.7 0.0 copy-start.7
  5.7 0.7 copy-done.7
  6.3 96.0 %shard_map.195 = (f32[256,1024]{1,0:T(8,128)S(1)}, f32[256,1024]{1,0:T(8,128)}, f32[256,1024]{1,0:T(8,128)}, f32[8,256]{1,0:T(8,128)S(1)}, f32[8,256]{1,0:T(8,12...) custom-call(bf16[2,2048,1024]{2,1,0:T(8,128)(2,1)} %bitcast.19, ...), custom_call_target="tpu_custom_call" | custom-call | tf_op jit(solution)/shard_map/pallas_call | solution.py:475
  102.3 0.0 copy-start.8
  102.4 1.0 copy.32
  103.3 3.0 %copy.33 = f32[256,1024]{1,0:T(8,128)} copy(f32[256,1024]{1,0:T(8,128)} %get-tuple-element.41) | data formatting | bytes 2097152
  106.3 2.3 %copy.34 = f32[256,1024]{1,0:T(8,128)} copy(f32[256,1024]{1,0:T(8,128)} %get-tuple-element.42) | data formatting | bytes 2097152
  108.6 0.6 copy.35
  109.2 0.6 copy.36
  109.8 0.6 copy.37
  110.4 0.6 copy.38
  111.0 0.6 copy.39
  111.6 0.6 copy.40
  112.1 0.0 copy-done.8
  112.1 2.0 %copy.41 = bf16[2048,1024]{1,0:T(8,128)(2,1)} copy(bf16[2048,1024]{1,0:T(8,128)(2,1)S(1)} %copy-done.8) | data formatting | bytes 8388608
Async XLA Ops:
  0.6 0.8 copy-start
  1.5 0.7 copy-start.1
  2.2 0.7 copy-start.2
  2.9 0.7 copy-start.3
  3.6 0.7 copy-start.4
  4.3 0.7 copy-start.5
  5.0 0.7 copy-start.6
  5.7 0.7 copy-start.7
  102.3 9.8 %copy-start.8 = (bf16[2048,1024]{1,0:T(8,128)(2,1)S(1)}, bf16[2048,1024]{1,0:T(8,128)(2,1)}, u32[]{:S(2)}) copy-start(bf16[2048,1024]{1,0:T(8,128)(2,1)} %get-tuple-element.49) | copy-start | bytes 12582916

commit v2 on v1

--- a/solution.py
+++ b/solution.py
@@ -28,14 +28,26 @@
     return (master_new, first_new, second_new)
 
 
-def encode(x):
-    return ((x * jnp.abs(x)) * (x * x)).astype(jnp.bfloat16)
-
-
-def decode(code):
+EDGE = 2.0**-8
+JOINT = 2.0**-48
+
+
+def encode(x, k):
+    size = jnp.abs(x) * 2.0**-k
+    second = size * size
+    fourth = second * second
+    code = jnp.where(size >= EDGE, fourth * fourth, second * JOINT)
+    return jnp.where(x < 0, -code, code).astype(jnp.bfloat16)
+
+
+def decode(code, k):
     y = code.astype(jnp.float32)
     size = jnp.abs(y)
-    x = lax.rsqrt(lax.rsqrt(size))
+    root = lax.rsqrt(size)
+    fourth = lax.rsqrt(root)
+    high = fourth * lax.rsqrt(fourth) * 2.0**k
+    low = size * root * (JOINT**-0.5 * 2.0**k)
+    x = jnp.where(size >= EDGE**8, high, low)
     x = jnp.where(y < 0, -x, x)
     return jnp.where(size < 2e-38, 0.0, x)
 
@@ -54,25 +66,24 @@
 def orders(shard_bits, replica_bits):
     shards = [("shard", j) for j in range(shard_bits)]
     replicas = [("replica", j) for j in range(replica_bits)]
-    one = [replicas[0], shards[0]] + replicas[1:] + shards[1:]
+    one = [replicas[0]] + shards[:2] + replicas[1:] + shards[2:]
     two = replicas + shards
     return (one, two)
 
 
 def kernel(
     shards, replicas,
-    kv_grads, router_grads, gain_grads, master, first, second,
-    r_master, r_first, r_second, g_master, g_first, g_second,
-    master_out, first_out, second_out, rm_out, rf_out, rs_out, gm_out, gf_out, gs_out, full,
-    slabs, acc, outgoing, incoming, whole_sum, own,
-    small, small_in, small_out, square_out, square_in,
-    load_sem, cut_send, cut_recv, small_send, small_recv, join_send, join_recv,
-    square_send, square_recv, up_sem, down_sem, x_sem, pair_sem, local_sem,
+    kv_grads, router_grads, gain_grads, master_in, first_in, second_in,
+    kv_gradient, small_gradient, full,
+    slabs, acc, outgoing, incoming, whole_sum, own, master, first, second, routers, gain_rows,
+    small, small_in, small_out, square_r, square_s,
+    load_sem, state_sem, cut_send, cut_recv, small_send, small_recv, join_send, join_recv,
+    square_r_sem, square_s_sem, up_sem, down_sem, x_sem, pair_sem, local_sem,
 ):
     s, r = lax.axis_index("shard"), lax.axis_index("replica")
     rows, columns = master.shape
     width = columns // (CHUNKS * replicas)
-    small_width = r_master.shape[1]
+    small_width = small.shape[2]
     shard_bits, replica_bits = shards.bit_length() - 1, replicas.bit_length() - 1
     bits = shard_bits + replica_bits
     blocks = shards * replicas
@@ -100,26 +111,42 @@
 
     pl.loop(0, shards)(lambda offset: load(offset).start())
 
+    def fetch(i):
+        pairs = (
+            (router_grads, routers), (gain_grads, gain_rows),
+            (master_in, master), (first_in, first), (second_in, second),
+        )
+        return pltpu.make_async_copy(pairs[i][0], pairs[i][1], state_sem.at[i])
+
+    for i in range(5):
+        fetch(i).start()
+
     lines = shards // 2
     z, x = lax.div(s, 2), lax.rem(s, 2)
+    above, below = {"shard": s + 2, "replica": r}, {"shard": s - 2, "replica": r}
+
+    def shard_peer(d):
+        return {"shard": lax.rem(s + d, shards), "replica": r}
+
+    def replica_peer(d):
+        return {"shard": s, "replica": lax.rem(r + d, replicas)}
+
     barrier = pltpu.get_barrier_semaphore()
-    for axis, j in plan[0]:
+
+    def greet(device):
         pl.semaphore_signal(
-            barrier, inc=1, device_id=partner(axis, j), device_id_type=pl.DeviceIdType.MESH
-        )
-    above, below = {"shard": s + 2, "replica": r}, {"shard": s - 2, "replica": r}
-
-    @pl.when(z < lines - 1)
-    def _():
-        pl.semaphore_signal(barrier, inc=1, device_id=above, device_id_type=pl.DeviceIdType.MESH)
-
-    @pl.when(z > 0)
-    def _():
-        pl.semaphore_signal(barrier, inc=1, device_id=below, device_id_type=pl.DeviceIdType.MESH)
+            barrier, inc=1, device_id=device, device_id_type=pl.DeviceIdType.MESH
+        )
+
+    pl.loop(1, replicas)(lambda d: greet(replica_peer(d)))
+    pl.loop(1, shards)(lambda d: greet(shard_peer(d)))
 
     def column_of(chunk, offset):
         owner = flipped(r, offset, replica_bits)
-        return pl.ds(pl.multiple_of((chunk * replicas + owner) * width, width), width)
+        at = lax.rem(owner, 2) * (columns // 2) + (
+            chunk * (replicas // 2) + lax.div(owner, 2)
+        ) * width
+        return pl.ds(pl.multiple_of(at, width), width)
 
     def place(chunk, shard_offset, replica_offset):
         out = 0
@@ -129,8 +156,10 @@
             )
         return out
 
-    def prepare(chunk, sent):
+    def prepare(chunk, sent, arriving=False):
         def body(offset):
+            if arriving:
+                load(offset).wait()
             for q in range(replicas):
                 if q % 2 != sent:
                     continue
@@ -141,7 +170,7 @@
                         offset, 1, piece, cols
                     ].astype(jnp.float32)
                     if sent:
-                        outgoing[chunk, at, piece, :] = encode(value)
+                        outgoing[chunk, at, piece, :] = encode(value, 0)
                     else:
                         acc[chunk, at, piece, :] = value
 
@@ -155,11 +184,8 @@
             cut_send.at[chunk, k], cut_recv.at[chunk, k], partner(axis, j),
         )
 
-    pl.loop(0, shards)(lambda offset: load(offset).wait())
-    prepare(0, 1)
-    pl.semaphore_wait(
-        barrier, bits + jnp.where(z < lines - 1, 1, 0) + jnp.where(z > 0, 1, 0)
-    )
+    prepare(0, 1, arriving=True)
+    pl.semaphore_wait(barrier, shards + replicas - 2)
     cut(0, 0).start()
     prepare(1, 1)
     cut(1, 0).start()
@@ -189,9 +215,11 @@
                 out = jnp.where(owner == i, total[:, i * small_width : (i + 1) * small_width], out)
             return out
 
-        small[at, 0:8, :] = taken(router_grads)
-        small[at, 8:10, :] = taken(gain_grads)
-
+        small[at, 0:8, :] = taken(routers)
+        small[at, 8:10, :] = taken(gain_rows)
+
+    fetch(0).wait()
+    fetch(1).wait()
     pl.loop(0, shards)(small_body)
 
     def small_copy(k):
@@ -220,12 +248,13 @@
         def send_body(i):
             for piece in pieces:
                 outgoing[chunk, i, piece, :] = encode(
-                    acc[chunk, i, piece, :] + decode(incoming[chunk, half + i, piece, :])
+                    acc[chunk, i, piece, :] + decode(incoming[chunk, half + i, piece, :], k),
+                    k + 1,
                 )
 
         def keep_body(i):
             for piece in pieces:
-                acc[chunk, i, piece, :] += decode(incoming[chunk, half + i, piece, :])
+                acc[chunk, i, piece, :] += decode(incoming[chunk, half + i, piece, :], k)
 
         if rest:
             pl.loop(rest, half)(send_body)
@@ -234,7 +263,7 @@
         else:
             for piece in pieces:
                 whole_sum[chunk, 0, piece, :] = acc[chunk, 0, piece, :] + decode(
-                    incoming[chunk, half, piece, :]
+                    incoming[chunk, half, piece, :], k
                 )
 
     def take_small(k):
@@ -280,36 +309,39 @@
             squares = squares + folded(value * value)
     small_sum = small_out[replica_bits]
     squares = squares + jnp.sum(small_sum * small_sum) * (1.0 / (replicas * 8 * 128))
-    square_out[0] = squares
-
-    def square_copy(k):
-        axis, j = small_plan[k]
+
+    def square_over_r(d):
         return remote(
-            square_out.at[k], square_in.at[k], square_send.at[k], square_recv.at[k],
-            partner(axis, j),
-        )
-
-    for k in range(bits):
-        square_copy(k).start()
-        square_copy(k).wait_recv()
-        square_out[k + 1] = square_out[k] + square_in[k]
+            square_r.at[r], square_r.at[r], square_r_sem.at[0, d], square_r_sem.at[1, d],
+            replica_peer(d),
+        )
+
+    def square_over_s(d):
+        return remote(
+            square_s.at[s], square_s.at[s], square_s_sem.at[0, d], square_s_sem.at[1, d],
+            shard_peer(d),
+        )
+
+    square_r[r] = squares
+    pl.loop(1, replicas)(lambda d: square_over_r(d).start())
+    pl.loop(1, replicas)(lambda d: square_over_r(d).wait_recv())
+    square_s[s] = jnp.sum(square_r[...], axis=0)
+    pl.loop(1, shards)(lambda d: square_over_s(d).start())
     for i in range(1, replica_bits):
         for chunk in range(CHUNKS):
             join(chunk, i - 1).wait_recv()
             join(chunk, i).start()
-
-    total = jnp.broadcast_to(jnp.sum(square_out[bits], keepdims=True), (8, 128))
+    for i in range(2, 5):
+        fetch(i).wait()
+    pl.loop(1, shards)(lambda d: square_over_s(d).wait_recv())
+
+    total = jnp.broadcast_to(
+        jnp.sum(jnp.sum(square_s[...], axis=0), keepdims=True), (8, 128)
+    )
     clip = jnp.minimum(
         1.0, jnp.sqrt(jnp.full((8, 128), PARAMS, jnp.float32)) / (jnp.sqrt(total) + 1e-06)
     )
     clip = clip[0:1, 0:1]
-
-    rm_out[...], rf_out[...], rs_out[...] = adamw(
-        r_master[...], r_first[...], r_second[...], clip * small_sum[0:8], 0.1
-    )
-    gm_out[...], gf_out[...], gs_out[...] = adamw(
-        g_master[...], g_first[...], g_second[...], clip * small_sum[8:10], 0.0
-    )
 
     def replica_offset(at):
         out = 0
@@ -317,61 +349,70 @@
             out = out + ((at >> i) % 2) * 2**j
         return out
 
+    for at in range(replicas // 2):
+        for chunk in range(CHUNKS):
+            q = replica_offset(at)
+            cols = column_of(chunk, q)
+            owner = flipped(r, q, replica_bits)
+            inside = (chunk * (replicas // 2) + lax.div(owner, 2)) * width
+            inside = pl.ds(pl.multiple_of(inside, width), width)
+            for piece in pieces:
+                new, _, _ = adamw(
+                    master[piece, cols], first[piece, cols], second[piece, cols],
+                    clip * whole_sum[chunk, at, piece, :], 0.1,
+                )
+                own[piece, inside] = new.astype(jnp.bfloat16)
+
+    side = lax.rem(r, 2)
+    half_columns = columns // 2
+    cols = pl.ds(pl.multiple_of(side * half_columns, half_columns), half_columns)
+    pair, across = partner("replica", 0), partner("shard", 0)
+
+    def block(zz, xx):
+        return full.at[pl.ds(pl.multiple_of((zz * 2 + xx) * rows, rows), rows), cols]
+
+    def up(t):
+        src = own if isinstance(t, int) else block(z - t, x)
+        return remote(src, block(z - t, x), up_sem.at[0, t], up_sem.at[1, t], above)
+
+    def down(t):
+        src = own if isinstance(t, int) else block(z + t, x)
+        return remote(src, block(z + t, x), down_sem.at[0, t], down_sem.at[1, t], below)
+
+    def cross(role, zz):
+        src = own if isinstance(role, int) else block(zz, x)
+        return remote(src, block(zz, x), x_sem.at[0, role], x_sem.at[1, role], across)
+
+    def to_pair(which, role, zz, xx):
+        src = own if isinstance(role, int) and which == 0 else block(zz, xx)
+        return remote(
+            src, block(zz, xx),
+            pair_sem.at[0, which, role], pair_sem.at[1, which, role], pair,
+        )
+
+    mine = pltpu.make_async_copy(own, block(z, x), local_sem)
+
+    @pl.when(z < lines - 1)
+    def _():
+        up(0).start()
+
+    @pl.when(z > 0)
+    def _():
+        down(0).start()
+
+    cross(0, z).start()
+    to_pair(0, 0, z, x).start()
+    mine.start()
+
+    small_gradient[...] = clip * small_sum
     for at in range(replicas):
         for chunk in range(CHUNKS):
             if at == replicas // 2:
                 join(chunk, replica_bits - 1).wait_recv()
-            cols = column_of(chunk, replica_offset(at))
+            gradient_cols = column_of(chunk, replica_offset(at))
             for piece in pieces:
-                new, first_new, second_new = adamw(
-                    master[piece, cols], first[piece, cols], second[piece, cols],
-                    clip * whole_sum[chunk, at, piece, :], 0.1,
-                )
-                master_out[piece, cols] = new
-                first_out[piece, cols] = first_new
-                second_out[piece, cols] = second_new
-                own[piece, cols] = new.astype(jnp.bfloat16)
-
-    side = lax.rem(r, 2)
-    half_columns = columns // 2
-    cols = pl.ds(pl.multiple_of(side * half_columns, half_columns), half_columns)
-    pair, across = partner("replica", 0), partner("shard", 0)
-
-    def block(zz, xx):
-        return full.at[pl.ds(pl.multiple_of((zz * 2 + xx) * rows, rows), rows), cols]
-
-    def up(t):
-        src = own.at[:, cols] if isinstance(t, int) else block(z - t, x)
-        return remote(src, block(z - t, x), up_sem.at[0, t], up_sem.at[1, t], above)
-
-    def down(t):
-        src = own.at[:, cols] if isinstance(t, int) else block(z + t, x)
-        return remote(src, block(z + t, x), down_sem.at[0, t], down_sem.at[1, t], below)
-
-    def cross(role, zz):
-        src = own.at[:, cols] if isinstance(role, int) else block(zz, x)
-        return remote(src, block(zz, x), x_sem.at[0, role], x_sem.at[1, role], across)
-
-    def to_pair(which, role, zz, xx):
-        return remote(
-            block(zz, xx), block(zz, xx),
-            pair_sem.at[0, which, role], pair_sem.at[1, which, role], pair,
-        )
-
-    mine = pltpu.make_async_copy(
-        own, full.at[pl.ds(pl.multiple_of(s * rows, rows), rows)], local_sem
-    )
-
-    @pl.when(z < lines - 1)
-    def _():
-        up(0).start()
-
-    @pl.when(z > 0)
-    def _():
-        down(0).start()
-
-    cross(0, z).start()
-    mine.start()
+                kv_gradient[piece, gradient_cols] = clip * whole_sum[chunk, at, piece, :]
+
     cross(0, z).wait_recv()
     to_pair(1, 0, z, 1 - x).start()
 
@@ -412,6 +453,7 @@
 
     mine.wait()
     cross(0, z).wait_send()
+    to_pair(0, 0, z, x).wait()
     to_pair(1, 0, z, 1 - x).wait()
 
     @pl.when(z < lines - 1)
@@ -448,10 +490,11 @@
         for chunk in range(CHUNKS):
             cut(chunk, k).wait_send()
         small_copy(k).wait_send()
-        square_copy(k).wait_send()
     for i in range(replica_bits):
         for chunk in range(CHUNKS):
             join(chunk, i).wait_send()
+    pl.loop(1, replicas)(lambda d: square_over_r(d).wait_send())
+    pl.loop(1, shards)(lambda d: square_over_s(d).wait_send())
 
 
 def on_device(
@@ -472,46 +515,57 @@
     shape = jax.ShapeDtypeStruct
     vmem, anywhere = pl.BlockSpec(memory_space=pltpu.VMEM), pl.BlockSpec(memory_space=pl.ANY)
     dma = pltpu.SemaphoreType.DMA
-    outs = pl.pallas_call(
+    state = pltpu.VMEM((rows, columns), f32)
+    kv_gradient, small_gradient, kv_full = pl.pallas_call(
         functools.partial(kernel, shards, replicas),
-        out_shape=[shape(kv_master.shape, f32)] * 3
-        + [shape(router_master.shape[::-1], f32)] * 3
-        + [shape(gains.shape, f32)] * 3
-        + [shape((rows * shards, columns), bf16)],
-        in_specs=[anywhere] + [vmem] * 11,
-        out_specs=[vmem] * 9 + [anywhere],
+        out_shape=[
+            shape(kv_master.shape, f32),
+            shape((16, small_width), f32),
+            shape((rows * shards, columns), bf16),
+        ],
+        in_specs=[anywhere] * 6,
+        out_specs=[vmem, vmem, anywhere],
         scratch_shapes=[
             pltpu.VMEM((shards, 2, rows, columns), bf16),
             pltpu.VMEM((CHUNKS, blocks // 2, rows, width), f32),
             pltpu.VMEM((CHUNKS, blocks, rows, width), bf16),
             pltpu.VMEM((CHUNKS, blocks, rows, width), bf16),
             pltpu.VMEM((CHUNKS, replicas, rows, width), f32),
-            pltpu.VMEM((rows, columns), bf16),
+            pltpu.VMEM((rows, columns // 2), bf16),
+            state, state, state,
+            pltpu.VMEM((2,) + router_grads.shape[:1:-1], bf16),
+            pltpu.VMEM(gain_grads.shape[1:], bf16),
             pltpu.VMEM((shards, 16, small_width), f32),
             pltpu.VMEM((shards + replica_bits, 16, small_width), f32),
             pltpu.VMEM((replica_bits + 1, 16, small_width), f32),
-            pltpu.VMEM((bits + 1, 8, 128), f32),
-            pltpu.VMEM((bits, 8, 128), f32),
-            dma((shards,)),
+            pltpu.VMEM((replicas, 8, 128), f32),
+            pltpu.VMEM((shards, 8, 128), f32),
+            dma((shards,)), dma((5,)),
             dma((CHUNKS, bits)), dma((CHUNKS, bits)),
             dma((bits,)), dma((bits,)),
             dma((CHUNKS, replica_bits)), dma((CHUNKS, replica_bits)),
-            dma((bits,)), dma((bits,)),
+            dma((2, replicas)), dma((2, shards)),
             dma((2, lines)), dma((2, lines)),
             dma((2, 2 * lines)),
             dma((2, 2, 2 * lines)),
             dma,
         ],
         compiler_params=pltpu.CompilerParams(
-            collective_id=0, has_side_effects=True, vmem_limit_bytes=52 * 2**20
+            collective_id=0, has_side_effects=True, vmem_limit_bytes=60 * 2**20
         ),
     )(
         kv_grads[0], router_grads[0].transpose(0, 2, 1), gain_grads[0],
         kv_master, kv_first, kv_second,
-        router_master.T, router_first.T, router_second.T,
-        gains, gains_first, gains_second,
-    )
-    return (*outs[:3], *(out.T for out in outs[3:6]), *outs[6:])
+    )
+    experts = router_master.shape[1]
+    kv = adamw(kv_master, kv_first, kv_second, kv_gradient, 0.1)
+    router = adamw(
+        router_master, router_first, router_second, small_gradient[:experts].T, 0.1
+    )
+    gain = adamw(
+        gains, gains_first, gains_second, small_gradient[experts : experts + 2], 0.0
+    )
+    return (*kv, *router, *gain, kv_full)
 
 
 def solution(mesh):

time: 115 us -> 95.4 us (0.83)
  local copies, waits for them, and re-layouts: 17.5 us -> 2.06 us
  Pallas kernels: 96 us -> 86 us
  other arithmetic: 0 us -> 6.33 us
    unnamed x28 -> x21, local copies, waits for them, and re-layouts: 17.5 us -> 2.06 us
    pallas_call x1, Pallas kernels: 96 us -> 86 us  [on_device(): pl.pallas_call(functools.partial(kernel, shards, replicas), out_shape=[sh...]
    sub x0 -> x3, other arithmetic: none -> 6.33 us  [adamw(): master_new = master - learning_rate * (direction + weight_decay * master)]
where the time goes in v2:
time: 95.4 us; the launch traced here: 95.2 us
  Pallas kernels  86 us (90%)
  other arithmetic  6.33 us (7%)
  local copies, waits for them, and re-layouts  2.06 us (2%)
    pallas_call x1, Pallas kernels, on_device(): pl.pallas_call(functools.partial(kernel, shards, replicas), out_shape=[sh...  86 us
    sub x3, other arithmetic, adamw(): master_new = master - learning_rate * (direction + weight_decay * master)  6.33 us
    unnamed x21, local copies, waits for them, and re-layouts  2.06 us

profile of v2, /device:TPU:0, one launch (start us, length us, event | category | flops | bytes accessed | tf_op | source)
XLA Modules:
  0.0 95.2 jit_solution(6703636534305238327)
XLA Ops:
  0.6 0.0 copy-start.7
  0.7 0.0 copy-start.8
  0.7 0.0 copy-start.9
  0.7 0.0 copy-start.4
  0.7 0.0 copy-start.5
  0.7 0.0 copy-start.6
  0.7 0.0 copy-start.1
  0.7 0.0 copy-start.2
  0.7 0.0 copy-start.3
  0.7 86.0 %shard_map.195 = (f32[256,1024]{1,0:T(8,128)}, f32[16,256]{1,0:T(8,128)}, bf16[2048,1024]{1,0:T(8,128)(2,1)}) custom-call(bf16[2,2048,1024]{2,1,0:T(8,128)(2,1)} %bitcast.12, bf16[2,8,2048]{2,1,0:T(8,128)(2,1)} %bitcast.13, bf16[2,2,2048]{2,1,0:T(2,128)(2,1)} %bitcast.14, f32[256,1024]{1,0:T(8,128)} %master_in.1, f32[256,1024]{1,0:T(8,128)} %first_in.1, ...), custom_call_target="tpu_custom_call" | custom-call | tf_op jit(solution)/shard_map/pallas_call | solution.py:519
  86.8 0.0 copy-start
  86.8 0.0 copy-done.7
  86.8 0.0 copy-done.8
  86.8 0.0 copy-done.9
  86.8 1.5 %multiply_subtract_fusion.2 = (f32[2,256]{1,0:T(2,128)}, f32[2,256]{1,0:T(2,128)}, f32[2,256]{1,0:T(2,128)}) fusion(f32[2,256]{1,0:T(2,128)S(1)} %copy-done.7, f32[16,256]{1,0:T(8,128)} %get-tuple-element.14, f32[2,256]{1,0:T(2,128)S(1)} %copy-done.8, f32[2,256]{1,0:T(2,128)S(1)} %copy-done.9), kind=kLoop, calls=%fused_computation.11 | loop fusion | flops 7680 | bytes 14336 | tf_op jit(solution)/shard_map/sub | solution.py:27
  88.2 0.0 copy-done.4
  88.2 0.0 copy-done.5
  88.3 0.0 copy-done.6
  88.3 1.3 %multiply_subtract_fusion.1 = (f32[256,8]{0,1:T(8,128)}, f32[256,8]{0,1:T(8,128)}, f32[256,8]{0,1:T(8,128)}) fusion(f32[256,8]{0,1:T(8,128)S(1)} %copy-done.4, f32[16,256]{1,0:T(8,128)} %get-tuple-element.14, f32[256,8]{0,1:T(8,128)S(1)} %copy-done.5, f32[256,8]{0,1:T(8,128)S(1)} %copy-done.6), kind=kLoop, calls=%fused_computation.8 | loop fusion | flops 30720 | bytes 57344 | tf_op jit(solution)/shard_map/sub | solution.py:27
  89.6 0.0 copy-done.1
  89.6 0.0 copy-done.2
  89.6 0.0 copy-done.3
  89.6 3.6 %multiply_subtract_fusion = (f32[256,1024]{1,0:T(8,128)}, f32[256,1024]{1,0:T(8,128)}, f32[256,1024]{1,0:T(8,128)}) fusion(f32[256,1024]{1,0:T(8,128)S(1)} %copy-done.1, f32[256,1024]{1,0:T(8,128)} %get-tuple-element.13, f32[256,1024]{1,0:T(8,128)S(1)} %copy-done.2, f32[256,1024]{1,0:T(8,128)S(1)} %copy-done.3), kind=kLoop, calls=%fused_computation.2 | loop fusion | flops 3932160 | bytes 7340032 | tf_op jit(solution)/shard_map/sub | solution.py:27
  93.1 0.0 copy-done
  93.1 2.0 %copy.23 = bf16[2048,1024]{1,0:T(8,128)(2,1)} copy(bf16[2048,1024]{1,0:T(8,128)(2,1)S(1)} %copy-done) | data formatting | bytes 8388608
Async XLA Ops:
  0.6 86.1 %copy-start.7 = (f32[2,256]{1,0:T(2,128)S(1)}, f32[2,256]{1,0:T(2,128)}, u32[]{:S(2)}) copy-start(f32[2,256]{1,0:T(2,128)} %param.21) | copy-start | bytes 6148
  0.7 86.1 %copy-start.8 = (f32[2,256]{1,0:T(2,128)S(1)}, f32[2,256]{1,0:T(2,128)}, u32[]{:S(2)}) copy-start(f32[2,256]{1,0:T(2,128)} %param.22) | copy-start | bytes 6148
  0.7 86.1 %copy-start.9 = (f32[2,256]{1,0:T(2,128)S(1)}, f32[2,256]{1,0:T(2,128)}, u32[]{:S(2)}) copy-start(f32[2,256]{1,0:T(2,128)} %param.23) | copy-start | bytes 6148
  0.7 87.6 %copy-start.4 = (f32[256,8]{0,1:T(8,128)S(1)}, f32[256,8]{0,1:T(8,128)}, u32[]{:S(2)}) copy-start(f32[256,8]{0,1:T(8,128)} %param.18) | copy-start | bytes 24580
  0.7 87.6 %copy-start.5 = (f32[256,8]{0,1:T(8,128)S(1)}, f32[256,8]{0,1:T(8,128)}, u32[]{:S(2)}) copy-start(f32[256,8]{0,1:T(8,128)} %param.19) | copy-start | bytes 24580
  0.7 87.6 %copy-start.6 = (f32[256,8]{0,1:T(8,128)S(1)}, f32[256,8]{0,1:T(8,128)}, u32[]{:S(2)}) copy-start(f32[256,8]{0,1:T(8,128)} %param.20) | copy-start | bytes 24580
  0.7 88.9 %copy-start.1 = (f32[256,1024]{1,0:T(8,128)S(1)}, f32[256,1024]{1,0:T(8,128)}, u32[]{:S(2)}) copy-start(f32[256,1024]{1,0:T(8,128)} %master_in.1) | copy-start | bytes 3145732
  0.7 88.9 %copy-start.2 = (f32[256,1024]{1,0:T(8,128)S(1)}, f32[256,1024]{1,0:T(8,128)}, u32[]{:S(2)}) copy-start(f32[256,1024]{1,0:T(8,128)} %first_in.1) | copy-start | bytes 3145732
  0.7 88.9 %copy-start.3 = (f32[256,1024]{1,0:T(8,128)S(1)}, f32[256,1024]{1,0:T(8,128)}, u32[]{:S(2)}) copy-start(f32[256,1024]{1,0:T(8,128)} %second_in.1) | copy-start | bytes 3145732
  86.8 6.4 %copy-start = (bf16[2048,1024]{1,0:T(8,128)(2,1)S(1)}, bf16[2048,1024]{1,0:T(8,128)(2,1)}, u32[]{:S(2)}) copy-start(bf16[2048,1024]{1,0:T(8,128)(2,1)} %get-tuple-element.44) | copy-start | bytes 12582916
